TPU v7x, 32 devices: a whole 2x2x4 slice. The times are simulated.
32 devices in a mesh: groups: 2 (over y), dp: 4 (over x, core), expert: 4 (over z).
Axes of the slice: x: 2, y: 2, z: 4, core: 2. Of those that a mesh axis runs over, the one named last changes fastest.
Arguments:
- tokens: bfloat16 [1024, 3072], P(('groups', 'dp'), 'expert'), parts along dimension 0, may hold values from -6 to 6
- cotangent: bfloat16 [1024, 3072], P(('groups', 'dp'), 'expert'), parts along dimension 0, may hold values from -6 to 6
- routes: int32 [1024, 2], P(('groups', 'dp')), parts along dimension 0, may hold values from 0 to 3, all different within a row; in each aligned block of 128 rows (0 to 127, 128 to 255, ...) at most 64 rows name the same one
- route_weight: float32 [1024, 2], P(('groups', 'dp')), parts along dimension 0, may hold values from 0.2 to 1
- tenant: int32 [1024], P(('groups', 'dp')), parts along dimension 0, may hold values from 0 to 1
- w_gate: bfloat16 [4, 3072, 8192], P('dp', None, 'expert'), may hold values from -0.109375 to 0.109375
- w_up: bfloat16 [4, 3072, 8192], P('dp', None, 'expert'), may hold values from -0.109375 to 0.109375
- w_down: bfloat16 [4, 8192, 3072], P('dp', 'expert'), may hold values from -0.0625 to 0.0625
- a_up: bfloat16 [4, 3072, 64], P('dp', 'expert'), may hold values from -0.109375 to 0.109375
- b_up: bfloat16 [4, 64, 8192], P('dp', None, 'expert'), may hold values from -1 to 1
- a_down: bfloat16 [4, 8192, 64], P('dp', 'expert'), may hold values from -0.0625 to 0.0625
- b_down: bfloat16 [4, 64, 3072], P('dp', None, 'expert'), may hold values from -1 to 1
Outputs:
- mixed: bfloat16 [1024, 3072], P(('groups', 'dp'), 'expert'), parts along dimension 0
- grad_a_up: float32 [8, 3072, 64], P(('groups', 'dp'), 'expert'), parts along dimension 0
- grad_b_up: float32 [8, 64, 8192], P(('groups', 'dp'), None, 'expert'), parts along dimension 0
- grad_a_down: float32 [8, 8192, 64], P(('groups', 'dp'), 'expert'), parts along dimension 0
- grad_b_down: float32 [8, 64, 3072], P(('groups', 'dp'), None, 'expert'), parts along dimension 0
There are 2 independent parts, one for each index of `groups`. A program takes and returns all parts, laid end to end along the dimension named above; an argument that names none is the same for every part. Nothing has to cross between parts.
Inputs may be any that keep to these rules, and one draw needn't show every extreme that they name: `routes`: each token names 2 different experts. Within the 128 tokens of one index of dp (aligned blocks of rows) no expert is named more than 64 times, and in some block some expert is named exactly 64 times.
All inputs are finite; a program needn't handle non-finite values.
Results may differ from a plain program's by a relative error of at most 0.006.
Values may be sent and summed in bfloat16 or wider, within the bound.
A program may use at most 128 MiB of HBM per device.

v0:
```python
import jax
import jax.numpy as jnp
from jax import lax
from jax.sharding import PartitionSpec as P

TOP = 2
RANK = 32
TENANTS = 2
CAP = 64


adapter_scale = 0.5


def slot_table(route_rows, expert_count, slot_count):
    flat = route_rows.reshape(-1)
    order = jnp.arange(flat.shape[0], dtype=jnp.int32)
    earlier = (flat[:, None] == flat[None, :]) & (order[None, :] < order[:, None])
    rank = jnp.sum(earlier.astype(jnp.int32), axis=1)
    expert_ids = jnp.arange(expert_count, dtype=jnp.int32)
    slot_ids = jnp.arange(slot_count, dtype=jnp.int32)
    picked = (flat[None, None, :] == expert_ids[:, None, None]) & (
        rank[None, None, :] == slot_ids[None, :, None]
    )
    return picked.astype(jnp.bfloat16)


def on_device(
    tokens,
    cotangent,
    routes,
    route_weight,
    tenant,
    w_gate,
    w_up,
    w_down,
    a_up,
    b_up,
    a_down,
    b_down,
):
    tok_count = tokens.shape[0]
    dwidth = tokens.shape[1]
    expert_count = lax.axis_size("dp")
    col_start = lax.axis_index("expert") * dwidth
    slot_pick = slot_table(routes, expert_count, CAP)
    token_rep = jnp.repeat(tokens, TOP, axis=0)
    dout_rep = (
        jnp.repeat(cotangent, TOP, axis=0).astype(jnp.float32) * route_weight.reshape(-1)[:, None]
    ).astype(jnp.bfloat16)
    tenant_hot = (tenant[:, None] == jnp.arange(TENANTS, dtype=jnp.int32)[None, :]).astype(
        jnp.bfloat16
    )
    hot_rep = jnp.repeat(tenant_hot, TOP, axis=0)
    send_x = jnp.einsum(
        "esp,pd->esd", slot_pick, token_rep, preferred_element_type=jnp.float32
    ).astype(jnp.bfloat16)
    send_do = jnp.einsum(
        "esp,pd->esd", slot_pick, dout_rep, preferred_element_type=jnp.float32
    ).astype(jnp.bfloat16)
    send_hot = jnp.einsum(
        "esp,pt->est", slot_pick, hot_rep, preferred_element_type=jnp.float32
    ).astype(jnp.bfloat16)
    got_x, got_do, got_hot = (
        lax.all_to_all(send_x, "dp", split_axis=0, concat_axis=0, tiled=True),
        lax.all_to_all(send_do, "dp", split_axis=0, concat_axis=0, tiled=True),
        lax.all_to_all(send_hot, "dp", split_axis=0, concat_axis=0, tiled=True),
    )
    local_rows = got_x.shape[0] * got_x.shape[1]
    rows_own = got_x.reshape(local_rows, dwidth)
    owned_output_gradient = got_do.reshape(local_rows, dwidth)
    hot_in = got_hot.reshape(local_rows, TENANTS)
    incoming_rows, incoming_output_gradient = (
        lax.all_gather(rows_own, "expert", axis=1, tiled=True),
        lax.all_gather(owned_output_gradient, "expert", axis=1, tiled=True),
    )
    gate_w = w_gate[0]
    up_weight_matrix = w_up[0]
    down_w = w_down[0]
    aup_w = a_up[0]
    up_adapter_weight = b_up[0]
    adown_w = a_down[0]
    down_adapter_weight = b_down[0]
    routing_mask = jnp.repeat(hot_in.astype(jnp.float32), RANK, axis=1)
    apart = jnp.dot(rows_own, aup_w, preferred_element_type=jnp.float32)
    partial_gradient = adapter_scale * jnp.dot(
        owned_output_gradient, down_adapter_weight.T, preferred_element_type=jnp.float32
    )
    a_total, d_total = lax.psum((apart, partial_gradient), "expert")
    lowrank_input_rows = (a_total * routing_mask).astype(jnp.bfloat16)
    lowrank_down_gradient = (d_total * routing_mask).astype(jnp.bfloat16)
    gate_pre = jnp.dot(incoming_rows, gate_w, preferred_element_type=jnp.float32)
    combined_up_product = jnp.dot(
        incoming_rows, up_weight_matrix, preferred_element_type=jnp.float32
    ) + adapter_scale * jnp.dot(
        lowrank_input_rows, up_adapter_weight, preferred_element_type=jnp.float32
    )
    gate_act = jax.nn.silu(gate_pre)
    hidden = (gate_act * combined_up_product).astype(jnp.bfloat16)
    c_total = lax.psum(jnp.dot(hidden, adown_w, preferred_element_type=jnp.float32), "expert")
    lowrank_cotangent = (c_total * routing_mask).astype(jnp.bfloat16)
    adapter_side_product = adapter_scale * jnp.dot(
        lowrank_cotangent, down_adapter_weight, preferred_element_type=jnp.float32
    )
    part = jnp.dot(hidden, down_w, preferred_element_type=jnp.float32)
    inner = lax.dynamic_slice_in_dim(part, col_start, dwidth, 1) + adapter_side_product
    whole_term = lax.dynamic_update_slice_in_dim(part, inner, col_start, 1)
    own_cols = lax.psum_scatter(whole_term, "expert", scatter_dimension=1, tiled=True).astype(
        jnp.bfloat16
    )
    back = lax.all_to_all(own_cols, "dp", split_axis=0, concat_axis=0, tiled=True)
    back = back.reshape(expert_count, CAP, dwidth)
    picked = jnp.einsum("esp,esd->pd", slot_pick, back, preferred_element_type=jnp.float32)
    mixed = jnp.sum(
        picked.reshape(tok_count, TOP, dwidth) * route_weight[:, :, None], axis=1
    ).astype(jnp.bfloat16)
    dhid_full = jnp.dot(
        incoming_output_gradient, down_w.T, preferred_element_type=jnp.float32
    ) + jnp.dot(lowrank_down_gradient, adown_w.T, preferred_element_type=jnp.float32)
    hidden_gradient = (dhid_full * gate_act).astype(jnp.bfloat16)
    down_adapter_gradient = adapter_scale * jnp.dot(
        lowrank_cotangent.T, owned_output_gradient, preferred_element_type=jnp.float32
    )
    grad_ad = jnp.dot(hidden.T, lowrank_down_gradient, preferred_element_type=jnp.float32)
    up_adapter_gradient = adapter_scale * jnp.dot(
        lowrank_input_rows.T, hidden_gradient, preferred_element_type=jnp.float32
    )
    projected_partial = (
        adapter_scale
        * jnp.dot(hidden_gradient, up_adapter_weight.T, preferred_element_type=jnp.float32)
        * routing_mask
    )
    cols_in = incoming_rows.astype(jnp.float32)
    grad_au = lax.psum_scatter(
        jnp.einsum("rd,rk->dk", cols_in, projected_partial, precision=lax.Precision.HIGHEST),
        "expert",
        scatter_dimension=0,
        tiled=True,
    )
    return (
        mixed,
        grad_au[None],
        up_adapter_gradient[None],
        grad_ad[None],
        down_adapter_gradient[None],
    )


def solution(mesh):
    return jax.shard_map(
        on_device,
        mesh=mesh,
        in_specs=(
            P(("groups", "dp"), "expert"),
            P(("groups", "dp"), "expert"),
            P(("groups", "dp"), None),
            P(("groups", "dp"), None),
            P(("groups", "dp")),
            P("dp", None, "expert"),
            P("dp", None, "expert"),
            P("dp", "expert", None),
            P("dp", "expert", None),
            P("dp", None, "expert"),
            P("dp", "expert", None),
            P("dp", None, "expert"),
        ),
        out_specs=(
            P(("groups", "dp"), "expert"),
            P(("groups", "dp"), "expert", None),
            P(("groups", "dp"), None, "expert"),
            P(("groups", "dp"), "expert", None),
            P(("groups", "dp"), None, "expert"),
        ),
        check_vma=False,
    )
```

profile of v0, /device:TPU:1, one launch (start us, length us, event | category | flops | bytes accessed | tf_op | source)
XLA Modules:
  0.0 277.7 jit_solution(11952199021366602191)
XLA Ops:
  8.4 1.2 broadcast_in_dim.32
  10.0 10.5 %all_to_all.24 = bf16[4,64,768]{2,1,0:T(8,128)(2,1)S(1)} all-to-all(bf16[4,64,768]{2,1,0:T(8,128)(2,1)S(1)} %convolution_convert_fusion.1), channel_id=1, replica_groups=mesh['groups'=2,'dp'=4,'expert'=4] {'dp'}, dimensions={0} | all-to-all | bytes 786432 | tf_op jit(solution)/shard_map/all_to_all | solution.py:65
  20.5 0.9 fusion.46
  23.2 4.2 %all-to-all-start.1 = ((bf16[4,64,2]{1,2,0:T(2,128)(2,1)}), bf16[4,64,2]{1,2,0:T(2,128)(2,1)S(1)}, u32[]{:S(2)}, u32[]{:S(2)}) async-start(bf16[4,64,2]{1,2,0:T(2,128)(2,1)} %convolution_convert_fusion.2), calls=%async_computation.1 | async-start | bytes 4096 | tf_op jit(solution)/shard_map/all_to_all | solution.py:67
  28.5 1.1 convolution_convert_fusion
  29.6 1.0 all-to-all-done.1
  30.6 4.0 %all-to-all-start.3 = ((bf16[4,64,768]{2,1,0:T(8,128)(2,1)}), bf16[4,64,768]{2,1,0:T(8,128)(2,1)S(1)}, u32[]{:S(2)}, u32[]{:S(2)}) async-start(bf16[4,64,768]{2,1,0:T(8,128)(2,1)} %convolution_convert_fusion), calls=%async_computation.4 | async-start | bytes 786432 | tf_op jit(solution)/shard_map/all_to_all | solution.py:66
  34.7 6.5 %all-to-all-done.3 = bf16[4,64,768]{2,1,0:T(8,128)(2,1)S(1)} async-done(((bf16[4,64,768]{2,1,0:T(8,128)(2,1)}), bf16[4,64,768]{2,1,0:T(8,128)(2,1)S(1)}, u32[]{:S(2)}, u32[]{:S(2)}) %all-to-all-start.3) | async-done | bytes 393248 | tf_op jit(solution)/shard_map/all_to_all | solution.py:66
  41.1 0.9 convolution_multiply_fusion.5
  42.0 12.3 %all-reduce.4.cloned.1.call-done = f32[256,64]{0,1:T(8,128)} async-done(((f32[256,64]{0,1:T(8,128)}), f32[256,64]{0,1:T(8,128)}) %all-reduce.4.cloned.1.call-update) | async-done | bytes 65552 | tf_op jit(solution)/shard_map/psum | solution.py:89
  54.3 0.8 fusion.48
  55.2 40.0 %all-gather.3.cloned.1.call-done = bf16[256,3072]{1,0:T(8,128)(2,1)} async-done(((bf16[256,768]{1,0:T(8,128)(2,1)}), bf16[256,3072]{1,0:T(8,128)(2,1)}) %all-gather.3.cloned.1.call-update) | async-done | bytes 1572880 | tf_op jit(solution)/shard_map/all_gather | solution.py:74
  95.2 8.6 %divide_multiply_fusion = f32[256,2048]{1,0:T(8,128)S(1)} fusion(bf16[256,3072]{1,0:T(8,128)(2,1)} %all-gather.3.cloned.1.call-done, bf16[1,3072,2048]{2,1,0:T(8,128)(2,1)} %param.17), kind=kOutput, calls=%fused_computation.18 | convolution fusion | flops 3223322624 | bytes 16252928 | tf_op jit(solution)/shard_map/dot_general | solution.py:92
  103.8 7.3 %fusion.4 = f32[256,2048]{1,0:T(8,128)S(1)} fusion(bf16[256,3072]{1,0:T(8,128)(2,1)S(1)} %copy-done.5, bf16[1,3072,2048]{2,1,0:T(8,128)(2,1)} %param.18), kind=kOutput, calls=%fused_computation.4 | convolution fusion | flops 3221225472 | bytes 16252928 | tf_op jit(solution)/shard_map/dot_general | solution.py:93
  111.6 1.1 fusion.30
  113.4 9.6 %fusion.2 = f32[256,3072]{1,0:T(8,128)} fusion(bf16[256,2048]{1,0:T(8,128)(2,1)S(1)} %fusion.12, bf16[1,2048,3072]{2,1,0:T(8,128)(2,1)} %param.19), kind=kOutput, calls=%fused_computation.2 | convolution fusion | flops 3221225472 | bytes 16777216 | tf_op jit(solution)/shard_map/dot_general | solution.py:105
  123.0 21.7 %all-reduce.6.cloned.1.call-done = (f32[256,64]{0,1:T(8,128)}, f32[256,64]{0,1:T(8,128)}) async-done(((f32[256,64]{0,1:T(8,128)}, f32[256,64]{0,1:T(8,128)}), (f32[256,64]{0,1:T(8,128)}, f32[256,64]{0,1:T(8,128)})) %all-reduce.6.cloned.1.call-update) | async-done | bytes 131088 | tf_op jit(solution)/shard_map/psum | solution.py:100
  144.7 0.9 fusion.50
  145.5 2.3 fusion.18
  148.1 36.4 %all-gather.5.cloned.1.call-done = bf16[256,3072]{1,0:T(8,128)(2,1)} async-done(((bf16[256,768]{1,0:T(8,128)(2,1)}), bf16[256,3072]{1,0:T(8,128)(2,1)}) %all-gather.5.cloned.1.call-update) | async-done | bytes 1572880 | tf_op jit(solution)/shard_map/all_gather | solution.py:75
  184.6 6.9 %fusion = f32[256,2048]{1,0:T(8,128)S(1)} fusion(bf16[256,3072]{1,0:T(8,128)(2,1)} %all-gather.5.cloned.1.call-done, bf16[1,2048,3072]{2,1,0:T(8,128)(2,1)} %param.19), kind=kOutput, calls=%fused_computation | convolution fusion | flops 3221225472 | bytes 16252928 | tf_op jit(solution)/shard_map/dot_general | solution.py:117
  191.5 2.6 fusion.11
  194.5 1.8 fusion.51
  196.6 1.1 fusion.13
  197.7 48.1 %reduce-scatter.3.cloned.1.call-done = f32[256,768]{1,0:T(8,128)} async-done(((f32[256,3072]{1,0:T(8,128)}), f32[256,768]{1,0:T(8,128)}) %reduce-scatter.3.cloned.1.call-update) | async-done | bytes 786448 | tf_op jit(solution)/shard_map/reduce_scatter | solution.py:108
  245.8 1.9 convert_element_type.63
  247.8 4.3 %all-to-all-start.2 = ((bf16[4,64,768]{2,1,0:T(8,128)(2,1)}), bf16[4,64,768]{2,1,0:T(8,128)(2,1)S(1)}, u32[]{:S(2)}, u32[]{:S(2)}) async-start(bf16[4,64,768]{2,1,0:T(8,128)(2,1)} %bitcast.9), calls=%async_computation.3 | async-start | bytes 786432 | tf_op jit(solution)/shard_map/all_to_all | solution.py:111
  252.0 0.9 fusion.20
  252.9 1.1 convolution_bitcast_fusion
  254.0 4.7 %all-to-all-done.2 = bf16[4,64,768]{2,1,0:T(8,128)(2,1)S(1)} async-done(((bf16[4,64,768]{2,1,0:T(8,128)(2,1)}), bf16[4,64,768]{2,1,0:T(8,128)(2,1)S(1)}, u32[]{:S(2)}, u32[]{:S(2)}) %all-to-all-start.2) | async-done | bytes 393248 | tf_op jit(solution)/shard_map/all_to_all | solution.py:111
  258.7 1.0 fusion.19
  259.8 11.1 %reduce-scatter.5.cloned.1.call-done = f32[768,64]{0,1:T(8,128)} async-done(((f32[3072,64]{0,1:T(8,128)}), f32[768,64]{0,1:T(8,128)}) %reduce-scatter.5.cloned.1.call-update) | async-done | bytes 196624 | tf_op jit(solution)/shard_map/reduce_scatter | solution.py:134
  (64 shorter events, 6.5 us)
Async XLA Ops:
  7.2 104.4 %copy-start = (bf16[1,2048,64]{1,2,0:T(8,128)(2,1)S(1)}, bf16[1,2048,64]{1,2,0:T(8,128)(2,1)}, u32[]{:S(2)}) copy-start(bf16[1,2048,64]{1,2,0:T(8,128)(2,1)} %param.22) | copy-start | bytes 786436
  7.2 13.3 %copy-start.10 = (bf16[1,768,64]{1,2,0:T(8,128)(2,1)S(1)}, bf16[1,768,64]{1,2,0:T(8,128)(2,1)}, u32[]{:S(2)}) copy-start(bf16[1,768,64]{1,2,0:T(8,128)(2,1)} %param.20) | copy-start | bytes 294916
  7.2 15.0 %copy-start.13 = (s32[128]{0:T(128)S(1)}, s32[128]{0:T(128)}, u32[]{:S(2)}) copy-start(s32[128]{0:T(128)} %param.16) | copy-start | bytes 1540
  7.2 47.1 %all-reduce.4.cloned.1.call-start = ((), (), s32[]{:S(2)}) async-start(), calls=%async_computation.7 | async-start | bytes 131072 | tf_op jit(solution)/shard_map/psum | solution.py:89
  8.4 19.0 %copy-start.9 = (bf16[128,768]{1,0:T(8,128)(2,1)S(1)}, bf16[128,768]{1,0:T(8,128)(2,1)}, u32[]{:S(2)}) copy-start(bf16[128,768]{1,0:T(8,128)(2,1)} %param.13) | copy-start | bytes 589828
  20.5 1.0 copy-start.4
  20.5 7.7 %copy-start.12 = (f32[128,2]{0,1:T(2,128)S(1)}, f32[128,2]{0,1:T(2,128)}, u32[]{:S(2)}) copy-start(f32[128,2]{0,1:T(2,128)} %param.15) | copy-start | bytes 3076
  21.4 73.8 %all-gather.3.cloned.1.call-start = ((), (), s32[]{:S(2)}) async-start(), calls=%async_computation.6 | async-start | bytes 1966080 | tf_op jit(solution)/shard_map/all_gather | solution.py:74
  23.2 7.4 %all-to-all-start.1 = ((bf16[4,64,2]{1,2,0:T(2,128)(2,1)}), bf16[4,64,2]{1,2,0:T(2,128)(2,1)S(1)}, u32[]{:S(2)}, u32[]{:S(2)}) async-start(bf16[4,64,2]{1,2,0:T(2,128)(2,1)} %convolution_convert_fusion.2), calls=%async_computation.1 | async-start | bytes 4096 | tf_op jit(solution)/shard_map/all_to_all | solution.py:67
  27.7 13.5 %copy-start.8 = (bf16[1,64,768]{2,1,0:T(8,128)(2,1)S(1)}, bf16[1,64,768]{2,1,0:T(8,128)(2,1)}, u32[]{:S(2)}) copy-start(bf16[1,64,768]{2,1,0:T(8,128)(2,1)} %param.23) | copy-start | bytes 294916
  30.6 10.6 %all-to-all-start.3 = ((bf16[4,64,768]{2,1,0:T(8,128)(2,1)}), bf16[4,64,768]{2,1,0:T(8,128)(2,1)S(1)}, u32[]{:S(2)}, u32[]{:S(2)}) async-start(bf16[4,64,768]{2,1,0:T(8,128)(2,1)} %convolution_convert_fusion), calls=%async_computation.4 | async-start | bytes 786432 | tf_op jit(solution)/shard_map/all_to_all | solution.py:66
  34.6 110.1 %all-reduce.6.cloned.1.call-start = ((), (), s32[]{:S(2)}) async-start(), calls=%async_computation.11 | async-start | bytes 262144 | tf_op jit(solution)/shard_map/psum | solution.py:100
  41.1 62.7 %copy-start.2 = (bf16[4,64,768]{2,1,0:T(8,128)(2,1)}, bf16[4,64,768]{2,1,0:T(8,128)(2,1)S(1)}, u32[]{:S(2)}) copy-start(bf16[4,64,768]{2,1,0:T(8,128)(2,1)S(1)} %all-to-all-done.3) | copy-start | bytes 1179652
  95.2 8.6 %copy-start.5 = (bf16[256,3072]{1,0:T(8,128)(2,1)S(1)}, bf16[256,3072]{1,0:T(8,128)(2,1)}, u32[]{:S(2)}) copy-start(bf16[256,3072]{1,0:T(8,128)(2,1)} %all-gather.3.cloned.1.call-done) | copy-start | bytes 4718596
  103.8 7.3 %copy-start.1 = (f32[256,2048]{1,0:T(8,128)}, f32[256,2048]{1,0:T(8,128)S(1)}, u32[]{:S(2)}) copy-start(f32[256,2048]{1,0:T(8,128)S(1)} %divide_multiply_fusion) | copy-start | bytes 6291460
  103.8 7.3 %copy-start.7 = (bf16[1,64,2048]{2,1,0:T(8,128)(2,1)S(1)}, bf16[1,64,2048]{2,1,0:T(8,128)(2,1)}, u32[]{:S(2)}) copy-start(bf16[1,64,2048]{2,1,0:T(8,128)(2,1)} %param.21) | copy-start | bytes 786436
  112.7 71.8 %all-gather.5.cloned.1.call-start = ((), (), s32[]{:S(2)}) async-start(), calls=%async_computation.9 | async-start | bytes 1966080 | tf_op jit(solution)/shard_map/all_gather | solution.py:75
  113.3 132.5 %reduce-scatter.3.cloned.1.call-start = ((), (), s32[]{:S(2)}) async-start(), calls=%async_computation.8 | async-start | bytes 3932160 | tf_op jit(solution)/shard_map/reduce_scatter | solution.py:108
  147.9 122.9 %reduce-scatter.5.cloned.1.call-start = ((), (), s32[]{:S(2)}) async-start(), calls=%async_computation.10 | async-start | bytes 983040 | tf_op jit(solution)/shard_map/reduce_scatter | solution.py:134
  191.5 3.1 %copy-start.6 = (bf16[256,3072]{1,0:T(8,128)(2,1)S(1)}, bf16[256,3072]{1,0:T(8,128)(2,1)}, u32[]{:S(2)}) copy-start(bf16[256,3072]{1,0:T(8,128)(2,1)} %all-gather.3.cloned.1.call-done) | copy-start | bytes 4718596
  194.1 2.5 copy-start.11
  196.3 55.7 %copy-start.3 = (bf16[4,64,768]{2,1,0:T(8,128)(2,1)S(1)}, bf16[4,64,768]{2,1,0:T(8,128)(2,1)}, u32[]{:S(2)}) copy-start(bf16[4,64,768]{2,1,0:T(8,128)(2,1)} %copy-done.2) | copy-start | bytes 1179652
  247.8 11.0 %all-to-all-start.2 = ((bf16[4,64,768]{2,1,0:T(8,128)(2,1)}), bf16[4,64,768]{2,1,0:T(8,128)(2,1)S(1)}, u32[]{:S(2)}, u32[]{:S(2)}) async-start(bf16[4,64,768]{2,1,0:T(8,128)(2,1)} %bitcast.9), calls=%async_computation.3 | async-start | bytes 786432 | tf_op jit(solution)/shard_map/all_to_all | solution.py:111
Sparse Core Ops, SparseCore 0:
  21.6 32.7 all-reduce.3
  56.6 38.5 all-gather.2
  112.8 31.7 all-reduce.5
  146.1 38.4 all-gather.4
  186.7 59.0 reduce-scatter.2
  248.6 22.1 reduce-scatter.4
where the time goes:
time: 280 us; the launch traced here: 278 us
  waiting for transfers between devices  183 us (65%)
  matrix products  49.1 us (18%)
  between operations  14.4 us (5%)
  starting transfers between devices  12.9 us (5%)
  blocking collectives  10.5 us (4%)
  other arithmetic  3.9 us (1%)
  local copies, waits for them, and re-layouts  3.88 us (1%)
    reduce_scatter x1, waiting for transfers between devices, on_device(): lax.psum_scatter(whole_term, 'expert', scatter_dimension=1, tiled=True)  48.1 us
    all_gather x1, waiting for transfers between devices, on_device(): lax.all_gather(rows_own, 'expert', axis=1, tiled=True)  40 us
    all_gather x1, waiting for transfers between devices, on_device(): lax.all_gather(owned_output_gradient, 'expert', axis=1, tiled=True)  36.4 us
    psum x1, waiting for transfers between devices, on_device(): lax.psum(jnp.dot(hidden, adown_w, preferred_element_type=jnp.float32), 'e...  21.7 us
    psum x1, waiting for transfers between devices, on_device(): a_total, d_total = lax.psum((apart, partial_gradient), 'expert')  12.3 us
    reduce_scatter x1, waiting for transfers between devices, on_device(): lax.psum_scatter(jnp.einsum('rd,rk->dk', cols_in, projected_partial, prec...  11.1 us
    all_to_all x1, blocking collectives, on_device(): lax.all_to_all(send_x, 'dp', split_axis=0, concat_axis=0, tiled=True)  10.5 us
    dot_general x1, matrix products, on_device(): part = jnp.dot(hidden, down_w, preferred_element_type=jnp.float32)  9.65 us
  transfers between devices with their start and end apart: 9, of which 9 were waited for; matrix products, arithmetic and copies ran while one was open for 13% of the time, Pallas kernels for 0%

commit v1 on v0

--- a/solution.py
+++ b/solution.py
@@ -1,6 +1,10 @@
+import functools
+
 import jax
 import jax.numpy as jnp
 from jax import lax
+from jax.experimental import pallas as pl
+from jax.experimental.pallas import tpu as pltpu
 from jax.sharding import PartitionSpec as P
 
 TOP = 2
@@ -25,7 +29,7 @@
     return picked.astype(jnp.bfloat16)
 
 
-def on_device(
+def on_device_plain(
     tokens,
     cotangent,
     routes,
@@ -130,12 +134,9 @@
         * jnp.dot(hidden_gradient, up_adapter_weight.T, preferred_element_type=jnp.float32)
         * routing_mask
     )
-    cols_in = incoming_rows.astype(jnp.float32)
-    grad_au = lax.psum_scatter(
-        jnp.einsum("rd,rk->dk", cols_in, projected_partial, precision=lax.Precision.HIGHEST),
-        "expert",
-        scatter_dimension=0,
-        tiled=True,
+    projected = lax.psum(projected_partial, "expert")
+    grad_au = jnp.einsum(
+        "rd,rk->dk", rows_own.astype(jnp.float32), projected, precision=lax.Precision.HIGHEST
     )
     return (
         mixed,
@@ -144,6 +145,481 @@
         grad_ad[None],
         down_adapter_gradient[None],
     )
+
+
+NT = (((1,), (1,)), ((), ()))
+
+
+def mm(a, b):
+    return jnp.dot(a, b, preferred_element_type=jnp.float32)
+
+
+def mm_nt(a, b):
+    return lax.dot_general(a, b, NT, preferred_element_type=jnp.float32)
+
+
+def fused_kernel(
+    nz,
+    nd,
+    tok_ref,
+    cot_ref,
+    pick_ref,
+    slotw_ref,
+    tens_ref,
+    c0_ref,
+    c1_ref,
+    rw_ref,
+    wg_hbm,
+    wu_hbm,
+    wd_hbm,
+    aupt_ref,
+    bup_ref,
+    adnt_ref,
+    bdn_ref,
+    mixed_ref,
+    gaut_ref,
+    gbu_ref,
+    gadt_ref,
+    gbd_ref,
+    wg,
+    wu,
+    wd,
+    tokg,
+    cotg,
+    selx,
+    seld,
+    xbuf,
+    dbuf,
+    gate,
+    up,
+    hidden,
+    dhid,
+    outs,
+    back,
+    mixs,
+    mixr,
+    mixo,
+    tenr,
+    part,
+    wsem,
+    zsend,
+    zrecv,
+    dsend,
+    drecv,
+    tsend,
+    trecv,
+    psend,
+    precv,
+    osend,
+    orecv,
+    msend,
+    mrecv,
+):
+    z = lax.axis_index("expert")
+    d = lax.axis_index("dp")
+    width = tok_ref.shape[1]
+    rows = nd * CAP
+    ffl = gate.shape[1]
+    tile = 512 if ffl % 512 == 0 else 256
+    zs = [lax.rem(z + k, nz) for k in range(nz)]
+    zb = [lax.rem(z - k + nz, nz) for k in range(nz)]
+    ds_ = [lax.rem(d + k, nd) for k in range(nd)]
+    db = [lax.rem(d - k + nd, nd) for k in range(nd)]
+    pending = []
+
+    def remote(src, dst, ssem, rsem, dev):
+        return pltpu.make_async_remote_copy(
+            src_ref=src,
+            dst_ref=dst,
+            send_sem=ssem,
+            recv_sem=rsem,
+            device_id=dev,
+            device_id_type=pl.DeviceIdType.MESH,
+        )
+
+    def send(*args):
+        copy = remote(*args)
+        copy.start()
+        pending.append(copy)
+
+    def weight(i, s):
+        lo = pl.multiple_of(s * width, width)
+        if i == 0:
+            return pltpu.make_async_copy(wg_hbm.at[0, pl.ds(lo, width), :], wg.at[s], wsem.at[i, s])
+        if i == 1:
+            return pltpu.make_async_copy(wu_hbm.at[0, pl.ds(lo, width), :], wu.at[s], wsem.at[i, s])
+        return pltpu.make_async_copy(wd_hbm.at[0, :, pl.ds(lo, width)], wd.at[s], wsem.at[i, s])
+
+    weight(0, z).start()
+    weight(1, z).start()
+    barrier = pltpu.get_barrier_semaphore()
+    for k in range(1, nz):
+        pl.semaphore_signal(
+            barrier, inc=1, device_id={"expert": zs[k]}, device_id_type=pl.DeviceIdType.MESH
+        )
+    for k in range(1, nd):
+        pl.semaphore_signal(
+            barrier, inc=1, device_id={"dp": ds_[k]}, device_id_type=pl.DeviceIdType.MESH
+        )
+    pl.semaphore_wait(barrier, nz + nd - 2)
+
+    for k in range(1, nz):
+        send(tok_ref, tokg.at[z], zsend.at[0, k], zrecv.at[0, k], {"expert": zs[k]})
+    for k in range(1, nd):
+        send(tens_ref.at[ds_[k]], tenr.at[d], tsend.at[k], trecv.at[k], {"dp": ds_[k]})
+    for k in range(1, nz):
+        send(cot_ref, cotg.at[z], zsend.at[1, k], zrecv.at[1, k], {"expert": zs[k]})
+    for k in range(1, nz):
+        weight(0, zb[k]).start()
+        weight(1, zb[k]).start()
+    for k in range(nz):
+        weight(2, zs[(k + 1) % nz]).start()
+
+    def dispatch(which, j):
+        s = zb[j]
+        own, gathered, sel, buf = (
+            (tok_ref, tokg, selx, xbuf) if which == 0 else (cot_ref, cotg, seld, dbuf)
+        )
+        if j:
+            remote(
+                own, gathered.at[s], zsend.at[which, j], zrecv.at[which, j], {"expert": zs[j]}
+            ).wait_recv()
+            block = gathered[s]
+        else:
+            block = own[...]
+        for k in list(range(1, nd)) + [0]:
+            e = ds_[k]
+            picked = mm(pick_ref[e], block)
+            if which:
+                picked = picked * slotw_ref[e]
+            picked = picked.astype(jnp.bfloat16)
+            if k:
+                sel[j, e] = picked
+                send(
+                    sel.at[j, e],
+                    buf.at[s, d],
+                    dsend.at[which, j, k],
+                    drecv.at[which, j, k],
+                    {"dp": e},
+                )
+            else:
+                buf[s, d] = picked
+
+    def arrived(which, j):
+        s = zb[j]
+        sel, buf = (selx, xbuf) if which == 0 else (seld, dbuf)
+        for k in range(1, nd):
+            remote(
+                sel.at[j, ds_[k]],
+                buf.at[s, db[k]],
+                dsend.at[which, j, k],
+                drecv.at[which, j, k],
+                {"dp": ds_[k]},
+            ).wait_recv()
+        return s
+
+    def part_out(kind, value):
+        tot = jnp.where(ten() > 0.5, value[RANK:], value[:RANK])
+        part[kind, z] = tot
+        for k in range(1, nz):
+            send(
+                part.at[kind, z],
+                part.at[kind, z],
+                psend.at[kind, k],
+                precv.at[kind, k],
+                {"expert": zs[k]},
+            )
+
+    def part_in(kind, scale):
+        for k in range(1, nz):
+            remote(
+                part.at[kind, z],
+                part.at[kind, zb[k]],
+                psend.at[kind, k],
+                precv.at[kind, k],
+                {"expert": zs[k]},
+            ).wait_recv()
+        tot = part[kind, 0]
+        for i in range(1, nz):
+            tot = tot + part[kind, i]
+        tot = tot * scale
+        high = ten() > 0.5
+        return jnp.concatenate([jnp.where(high, 0.0, tot), jnp.where(high, tot, 0.0)], axis=0)
+
+    def ten():
+        tot = tenr[0, 0:1]
+        for i in range(1, nd):
+            tot = tot + tenr[i, 0:1]
+        return tot
+
+    def tiles(body):
+        def run(i, carry):
+            body(pl.ds(pl.multiple_of(i * tile, tile), tile))
+            return carry
+
+        lax.fori_loop(0, ffl // tile, run, 0)
+
+    def forward(j):
+        s = arrived(0, j)
+        weight(0, s).wait()
+        weight(1, s).wait()
+
+        def body(cols):
+            xs = xbuf[s].reshape(rows, width)
+            g = mm(xs, wg[s, :, cols])
+            u = mm(xs, wu[s, :, cols])
+            if j:
+                gate[:, cols] += g
+                up[:, cols] += u
+            else:
+                gate[:, cols] = g
+                up[:, cols] = u
+
+        tiles(body)
+
+    dispatch(0, 0)
+    tenr[d] = tens_ref[d]
+    for k in range(1, nd):
+        remote(
+            tens_ref.at[ds_[k]], tenr.at[db[k]], tsend.at[k], trecv.at[k], {"dp": ds_[k]}
+        ).wait_recv()
+    dispatch(0, 1)
+    forward(0)
+    part_out(0, mm_nt(aupt_ref[...], xbuf[z].reshape(rows, width)))
+    for j in range(2, nz):
+        dispatch(0, j)
+        forward(j - 1)
+    dispatch(1, 0)
+    forward(nz - 1)
+    low_a_t = part_in(0, 1.0)
+    low_a = low_a_t.T.astype(jnp.bfloat16)
+    low_a_t = low_a_t.astype(jnp.bfloat16)
+    dispatch(1, 1)
+
+    def act(cols):
+        g = gate[:, cols]
+        u = up[:, cols] + adapter_scale * mm(low_a, bup_ref[:, cols])
+        a = g / (1.0 + jnp.exp(-g))
+        gate[:, cols] = a
+        hidden[:, cols] = (a * u).astype(jnp.bfloat16)
+
+    tiles(act)
+    part_out(2, mm_nt(adnt_ref[...], hidden[...]))
+    dispatch(1, 2)
+
+    def down(k, low_c):
+        c = zs[k]
+        weight(2, c).wait()
+        for t in range(0, width, 256):
+            n = min(256, width - t)
+            r = mm(hidden[...], wd[c, :, t : t + n])
+            if k == 0:
+                r = r + adapter_scale * mm(low_c, bdn_ref[:, t : t + n])
+            outs[c, :, :, t : t + n] = r.astype(jnp.bfloat16).reshape(nd, CAP, n)
+        for i in range(1, nd):
+            send(
+                outs.at[c, ds_[i]], back.at[c, d], osend.at[k, i], orecv.at[k, i], {"dp": ds_[i]}
+            )
+        back[c, d] = outs[c, d]
+
+    def combine(k):
+        c = zs[k]
+        for i in range(1, nd):
+            remote(
+                outs.at[c, ds_[i]], back.at[c, db[i]], osend.at[k, i], orecv.at[k, i], {"dp": ds_[i]}
+            ).wait_recv()
+        b = back[c].reshape(rows, width)
+        m = mm(c0_ref[...], b) * rw_ref[:, 0:1] + mm(c1_ref[...], b) * rw_ref[:, 1:2]
+        if k:
+            mixs[c] = m.astype(jnp.bfloat16)
+            send(mixs.at[c], mixr.at[z], msend.at[k], mrecv.at[k], {"expert": c})
+        else:
+            mixo[...] = m
+
+    def backward(j, low_d):
+        s = arrived(1, j) if j else z
+
+        def body(cols):
+            r = mm_nt(dbuf[s].reshape(rows, width), wd[s, cols, :])
+            if j == 0:
+                up[:, cols] = r
+            elif j < nz - 1:
+                up[:, cols] += r
+            else:
+                r = r + up[:, cols] + mm(low_d, adnt_ref[:, cols])
+                dhid[:, cols] = (r * gate[:, cols]).astype(jnp.bfloat16)
+
+        tiles(body)
+
+    down(1, None)
+    for j in range(3, nz):
+        dispatch(1, j)
+    for k in range(2, nz):
+        down(k, None)
+    low_c_t = part_in(2, 1.0)
+    low_c = low_c_t.T.astype(jnp.bfloat16)
+    down(0, low_c)
+    arrived(1, 0)
+    part_out(1, mm_nt(bdn_ref[...], dbuf[z].reshape(rows, width)))
+    low_c_t = low_c_t.astype(jnp.bfloat16)
+    combine(1)
+    gbd_ref[...] = adapter_scale * mm(low_c_t, dbuf[z].reshape(rows, width))
+    return_steps = list(range(2, nz)) + [0]
+    low_d = None
+    for j in range(nz):
+        if j == nz - 1:
+            low_d_t = part_in(1, adapter_scale)
+            low_d = low_d_t.T.astype(jnp.bfloat16)
+            low_d_t = low_d_t.astype(jnp.bfloat16)
+        backward(j, low_d)
+        if j < len(return_steps):
+            combine(return_steps[j])
+    part_out(3, mm_nt(bup_ref[...], dhid[...]))
+
+    def grads(cols):
+        gadt_ref[:, cols] = mm(low_d_t, hidden[:, cols])
+        gbu_ref[:, cols] = adapter_scale * mm(low_a_t, dhid[:, cols])
+
+    tiles(grads)
+    low_z = part_in(3, adapter_scale)
+    hi = low_z.astype(jnp.bfloat16)
+    lo = (low_z - hi.astype(jnp.float32)).astype(jnp.bfloat16)
+    xs = xbuf[z].reshape(rows, width)
+    gaut_ref[...] = mm(hi, xs) + mm(lo, xs)
+    total = mixo[...]
+    for k in range(1, nz):
+        remote(mixs.at[zs[k]], mixr.at[zb[k]], msend.at[k], mrecv.at[k], {"expert": zs[k]}).wait_recv()
+        total = total + mixr[zb[k]].astype(jnp.float32)
+    mixed_ref[...] = total.astype(jnp.bfloat16)
+    for copy in pending:
+        copy.wait_send()
+
+
+def on_device_fused(
+    tokens,
+    cotangent,
+    routes,
+    route_weight,
+    tenant,
+    w_gate,
+    w_up,
+    w_down,
+    a_up,
+    b_up,
+    a_down,
+    b_down,
+):
+    nz, nd = lax.axis_size("expert"), lax.axis_size("dp")
+    tok_count, width = tokens.shape
+    ffl = w_gate.shape[2]
+    rows = nd * CAP
+    flat = routes.reshape(-1)
+    order = jnp.arange(flat.shape[0], dtype=jnp.int32)
+    earlier = (flat[:, None] == flat[None, :]) & (order[None, :] < order[:, None])
+    rank = jnp.sum(earlier.astype(jnp.int32), axis=1)
+    place = (flat * CAP + rank).reshape(tok_count, TOP)
+    slot = jnp.arange(rows, dtype=jnp.int32)
+    hit0 = place[None, :, 0] == slot[:, None]
+    hit1 = place[None, :, 1] == slot[:, None]
+    pick = (hit0 | hit1).astype(jnp.bfloat16).reshape(nd, CAP, tok_count)
+    slotw = jnp.sum(
+        jnp.where(hit0, route_weight[None, :, 0], 0.0)
+        + jnp.where(hit1, route_weight[None, :, 1], 0.0),
+        axis=1,
+    ).reshape(nd, CAP, 1)
+    slot_tenant = jnp.sum(
+        jnp.where(hit0 | hit1, tenant[None, :].astype(jnp.float32), 0.0), axis=1
+    ).reshape(nd, 1, 1, CAP)
+    mine = (jnp.arange(nd, dtype=jnp.int32) == lax.axis_index("dp")).astype(jnp.float32)
+    tens = jnp.broadcast_to(slot_tenant * mine[None, None, :, None], (nd, 8, nd, CAP)).reshape(
+        nd, 8, rows
+    )
+    c0 = (place[:, 0:1] == slot[None, :]).astype(jnp.bfloat16)
+    c1 = (place[:, 1:2] == slot[None, :]).astype(jnp.bfloat16)
+    vmem = pl.BlockSpec(memory_space=pltpu.VMEM)
+    hbm = pl.BlockSpec(memory_space=pl.ANY)
+    bf, f32 = jnp.bfloat16, jnp.float32
+    dma = pltpu.SemaphoreType.DMA
+    wide = TENANTS * RANK
+    mixed, gaut, gbu, gadt, gbd = pl.pallas_call(
+        functools.partial(fused_kernel, nz, nd),
+        out_shape=(
+            jax.ShapeDtypeStruct((tok_count, width), bf),
+            jax.ShapeDtypeStruct((wide, width), f32),
+            jax.ShapeDtypeStruct((wide, ffl), f32),
+            jax.ShapeDtypeStruct((wide, ffl), f32),
+            jax.ShapeDtypeStruct((wide, width), f32),
+        ),
+        in_specs=[vmem] * 8 + [hbm] * 3 + [vmem] * 4,
+        out_specs=[vmem] * 5,
+        scratch_shapes=[
+            pltpu.VMEM((nz, width, ffl), bf),
+            pltpu.VMEM((nz, width, ffl), bf),
+            pltpu.VMEM((nz, ffl, width), bf),
+            pltpu.VMEM((nz, tok_count, width), bf),
+            pltpu.VMEM((nz, tok_count, width), bf),
+            pltpu.VMEM((nz, nd, CAP, width), bf),
+            pltpu.VMEM((nz, nd, CAP, width), bf),
+            pltpu.VMEM((nz, nd, CAP, width), bf),
+            pltpu.VMEM((nz, nd, CAP, width), bf),
+            pltpu.VMEM((rows, ffl), f32),
+            pltpu.VMEM((rows, ffl), f32),
+            pltpu.VMEM((rows, ffl), bf),
+            pltpu.VMEM((rows, ffl), bf),
+            pltpu.VMEM((nz, nd, CAP, width), bf),
+            pltpu.VMEM((nz, nd, CAP, width), bf),
+            pltpu.VMEM((nz, tok_count, width), bf),
+            pltpu.VMEM((nz, tok_count, width), bf),
+            pltpu.VMEM((tok_count, width), f32),
+            pltpu.VMEM((nd, 8, rows), f32),
+            pltpu.VMEM((4, nz, RANK, rows), f32),
+            dma((3, nz)),
+            dma((2, nz)),
+            dma((2, nz)),
+            dma((2, nz, nd)),
+            dma((2, nz, nd)),
+            dma((nd,)),
+            dma((nd,)),
+            dma((4, nz)),
+            dma((4, nz)),
+            dma((nz, nd)),
+            dma((nz, nd)),
+            dma((nz,)),
+            dma((nz,)),
+        ],
+        compiler_params=pltpu.CompilerParams(
+            collective_id=0, has_side_effects=True, vmem_limit_bytes=62 * 1024 * 1024
+        ),
+    )(
+        tokens,
+        cotangent,
+        pick,
+        slotw,
+        tens,
+        c0,
+        c1,
+        route_weight,
+        w_gate,
+        w_up,
+        w_down,
+        a_up[0].T,
+        b_up[0],
+        a_down[0].T,
+        b_down[0],
+    )
+    return mixed, gaut.T[None], gbu[None], gadt.T[None], gbd[None]
+
+
+def on_device(*args):
+    nz, nd = lax.axis_size("expert"), lax.axis_size("dp")
+    tok_count, width = args[0].shape
+    ffl = args[5].shape[2]
+    weight_bytes = 6 * nz * width * ffl
+    row_bytes = 12 * nz * nd * CAP * width
+    fits = weight_bytes + row_bytes <= 50 * 1024 * 1024
+    if width % 128 or ffl % 256 or tok_count % 128 or (nd * CAP) % 128 or not fits:
+        return on_device_plain(*args)
+    return on_device_fused(*args)
 
 
 def solution(mesh):

time: 280 us -> 105 us (0.38)
  waiting for transfers between devices: 183 us -> 0 us
  Pallas kernels: 0 us -> 87.1 us
  matrix products: 49.1 us -> 0 us
  between operations: 14.4 us -> 0.68 us
  starting transfers between devices: 12.9 us -> 0 us
  blocking collectives: 10.5 us -> 0 us
  local copies, waits for them, and re-layouts: 3.88 us -> 13.7 us
    pallas_call x0 -> x1, Pallas kernels: none -> 87.1 us  [on_device_fused(): pl.pallas_call(functools.partial(fused_kernel, nz, nd), out_shape=(jax.Sh...]
    all_gather x2 -> x0, waiting for transfers between devices: 76.4 us -> none  [the longest x1 40 us: on_device(): lax.all_gather(rows_own, 'expert', axis=1, tiled=True)]
    reduce_scatter x2 -> x0, waiting for transfers between devices: 59.2 us -> none  [the longest x1 48.1 us: on_device(): lax.psum_scatter(whole_term, 'expert', scatter_dimension=1, tiled=True)]
    dot_general x19 -> x0, matrix products: 49.1 us -> none  [the longest x1 9.65 us: on_device(): part = jnp.dot(hidden, down_w, preferred_element_type=jnp.float32)]
    psum x2 -> x0, waiting for transfers between devices: 34 us -> none  [the longest x1 21.7 us: on_device(): lax.psum(jnp.dot(hidden, adown_w, preferred_element_type=jnp.float32), 'e...]
    all_to_all x3 -> x0, starting transfers between devices: 12.5 us -> none  [the longest x1 4.28 us: on_device(): lax.all_to_all(own_cols, 'dp', split_axis=0, concat_axis=0, tiled=True)]
    all_to_all x3 -> x0, waiting for transfers between devices: 12.2 us -> none  [the longest x1 6.48 us: on_device(): lax.all_to_all(send_do, 'dp', split_axis=0, concat_axis=0, tiled=True)]
    all_to_all x1 -> x0, blocking collectives: 10.5 us -> none  [on_device(): lax.all_to_all(send_x, 'dp', split_axis=0, concat_axis=0, tiled=True)]
  transfers between devices with their start and end apart: 9 -> 0, of which waited for: 9 -> 0; matrix products, arithmetic and copies ran while one was open for 13% -> 0% of each run, Pallas kernels for 0% -> 0%
where the time goes in v1:
time: 105 us
  Pallas kernels  87.1 us (83%)
  local copies, waits for them, and re-layouts  13.7 us (13%)
  other arithmetic  3.22 us (3%)
    pallas_call x1, Pallas kernels, on_device_fused(): pl.pallas_call(functools.partial(fused_kernel, nz, nd), out_shape=(jax.Sh...  87.1 us
    unnamed x7, local copies, waits for them, and re-layouts  10.8 us

profile of v1, /device:TPU:1, one launch (start us, length us, event | category | flops | bytes accessed | tf_op | source)
XLA Modules:
  0.0 104.6 jit_solution(6307842614179297510)
XLA Ops:
  0.6 0.7 convert_element_type.26
  1.3 0.8 slice_bitcast_fusion.1
  2.1 0.1 mul.38
  2.1 0.1 mul.39
  2.2 0.8 copy.33
  3.0 0.1 eq.105
  3.1 0.2 convert_reduce_fusion
  3.3 0.1 reduce_sum.30
  3.5 0.1 copy.34
  3.5 0.7 multiply_add_fusion.1
  4.3 0.2 select_reduce_fusion
  4.4 0.1 mul.35
  4.5 0.1 mul.37
  4.6 0.6 broadcast_in_dim.59.tens_ref
  5.2 0.7 or_convert_fusion.pick_ref
  6.0 1.4 %copy.36.rw_ref = f32[128,2]{1,0:T(8,128)} copy(f32[128,2]{0,1:T(2,128)} %param.15) | data formatting | bytes 2048 | tf_op args[3]
  7.4 0.8 fusion.2
  8.1 0.9 reshape.66.slotw_ref
  9.0 87.1 %shard_map.155 = (bf16[128,768]{1,0:T(8,128)(2,1)}, f32[64,768]{1,0:T(8,128)}, f32[64,2048]{1,0:T(8,128)}, f32[64,2048]{1,0:T(8,128)}, f32[64,768]{1,0:T(8,128)}) custom-call(bf16[128,768]{1,0:T(8,128)(2,1)} %tok_ref.1, bf16[128,768]{1,0:T(8,128)(2,1)} %cot_ref.1, bf16[4,64,128]{2,1,0:T(8,128)(2,1)} %or_convert_fusion.pick_ref, ...), custom_call_target="tpu_custom_call" | custom-call | tf_op jit(solution)/shard_map/pallas_call | solution.py:544
  96.0 1.6 %copy.42 = bf16[128,768]{1,0:T(8,128)(2,1)} copy(bf16[128,768]{1,0:T(8,128)(2,1)} %get-tuple-element.28) | data formatting | bytes 393216
  97.7 1.6 %copy.43 = f32[1,768,64]{1,2,0:T(8,128)} copy(f32[1,768,64]{1,2,0:T(8,128)} %bitcast.29) | data formatting | bytes 393216
  99.3 1.9 %copy.44 = f32[1,64,2048]{2,1,0:T(8,128)} copy(f32[1,64,2048]{2,1,0:T(8,128)} %bitcast.25) | data formatting | bytes 1048576
  101.1 1.9 %copy.45 = f32[1,2048,64]{1,2,0:T(8,128)} copy(f32[1,2048,64]{1,2,0:T(8,128)} %bitcast.24) | data formatting | bytes 1048576
  103.0 1.6 %copy.46 = f32[1,64,768]{2,1,0:T(8,128)} copy(f32[1,64,768]{2,1,0:T(8,128)} %bitcast.28) | data formatting | bytes 393216
  (5 shorter events, 0.0 us)

commit v2 on v1

--- a/solution.py
+++ b/solution.py
@@ -163,12 +163,9 @@
     nd,
     tok_ref,
     cot_ref,
-    pick_ref,
-    slotw_ref,
-    tens_ref,
-    c0_ref,
-    c1_ref,
+    route_ref,
     rw_ref,
+    tenant_ref,
     wg_hbm,
     wu_hbm,
     wd_hbm,
@@ -181,6 +178,12 @@
     gbu_ref,
     gadt_ref,
     gbd_ref,
+    pick_ref,
+    slotw_ref,
+    tens_ref,
+    c0_ref,
+    c1_ref,
+    rwc_ref,
     wg,
     wu,
     wd,
@@ -265,8 +268,6 @@
 
     for k in range(1, nz):
         send(tok_ref, tokg.at[z], zsend.at[0, k], zrecv.at[0, k], {"expert": zs[k]})
-    for k in range(1, nd):
-        send(tens_ref.at[ds_[k]], tenr.at[d], tsend.at[k], trecv.at[k], {"dp": ds_[k]})
     for k in range(1, nz):
         send(cot_ref, cotg.at[z], zsend.at[1, k], zrecv.at[1, k], {"expert": zs[k]})
     for k in range(1, nz):
@@ -274,6 +275,39 @@
         weight(1, zb[k]).start()
     for k in range(nz):
         weight(2, zs[(k + 1) % nz]).start()
+
+    toks = tok_ref.shape[0]
+    f32, bf = jnp.float32, jnp.bfloat16
+    lane = lax.broadcasted_iota(jnp.int32, (toks, toks), 1)
+    line = lax.broadcasted_iota(jnp.int32, (toks, toks), 0)
+    sooner = jnp.where(line < lane, 1.0, 0.0).astype(bf)
+    expert_id = lax.broadcasted_iota(jnp.int32, (toks, toks), 0)
+    hot = [jnp.where(expert_id == route_ref[k : k + 1, :], 1.0, 0.0) for k in range(TOP)]
+    count = mm(sum(hot).astype(bf), sooner)
+    slot_id = lax.broadcasted_iota(jnp.int32, (rows, toks), 0).astype(f32)
+    hits, slot_weight = [], 0.0
+    for k in range(TOP):
+        rank = jnp.sum(hot[k] * count, axis=0, keepdims=True)
+        place = route_ref[k : k + 1, :].astype(f32) * CAP + rank
+        hit = jnp.where((slot_id == place), 1.0, 0.0)
+        hits.append(hit)
+        weights = rw_ref[k : k + 1, :]
+        slot_weight = slot_weight + jnp.sum(hit * weights, axis=1, keepdims=True)
+        c_ref = (c0_ref, c1_ref)[k]
+        c_ref[...] = hit.T.astype(bf)
+        rwc_ref[k] = jnp.broadcast_to(weights, (toks, toks)).T
+    pick = (hits[0] + hits[1]).astype(bf)
+    pick_ref[...] = pick.reshape(nd, CAP, toks)
+    slotw_ref[...] = jnp.broadcast_to(slot_weight, (rows, toks)).reshape(nd, CAP, toks)
+    tenant_row = jnp.broadcast_to(tenant_ref[...].astype(f32), (8, toks)).astype(bf)
+    slot_tenant = mm(tenant_row, c0_ref[...]) + mm(tenant_row, c1_ref[...])
+    slot_lane = lax.broadcasted_iota(jnp.int32, (8, rows), 1)
+    mine = (slot_lane >= d * CAP) & (slot_lane < (d + 1) * CAP)
+    for k in range(nd):
+        turned = slot_tenant if k == 0 else pltpu.roll(slot_tenant, (nd - k) * CAP, 1)
+        tens_ref[k] = jnp.where(mine, turned, 0.0)
+    for k in range(1, nd):
+        send(tens_ref.at[k], tenr.at[d], tsend.at[k], trecv.at[k], {"dp": ds_[k]})
 
     def dispatch(which, j):
         s = zb[j]
@@ -291,7 +325,7 @@
             e = ds_[k]
             picked = mm(pick_ref[e], block)
             if which:
-                picked = picked * slotw_ref[e]
+                picked = picked * slotw_ref[e, :, 0:1]
             picked = picked.astype(jnp.bfloat16)
             if k:
                 sel[j, e] = picked
@@ -378,10 +412,10 @@
         tiles(body)
 
     dispatch(0, 0)
-    tenr[d] = tens_ref[d]
+    tenr[d] = tens_ref[0]
     for k in range(1, nd):
         remote(
-            tens_ref.at[ds_[k]], tenr.at[db[k]], tsend.at[k], trecv.at[k], {"dp": ds_[k]}
+            tens_ref.at[k], tenr.at[db[k]], tsend.at[k], trecv.at[k], {"dp": ds_[k]}
         ).wait_recv()
     dispatch(0, 1)
     forward(0)
@@ -429,7 +463,7 @@
                 outs.at[c, ds_[i]], back.at[c, db[i]], osend.at[k, i], orecv.at[k, i], {"dp": ds_[i]}
             ).wait_recv()
         b = back[c].reshape(rows, width)
-        m = mm(c0_ref[...], b) * rw_ref[:, 0:1] + mm(c1_ref[...], b) * rw_ref[:, 1:2]
+        m = mm(c0_ref[...], b) * rwc_ref[0, :, 0:1] + mm(c1_ref[...], b) * rwc_ref[1, :, 0:1]
         if k:
             mixs[c] = m.astype(jnp.bfloat16)
             send(mixs.at[c], mixr.at[z], msend.at[k], mrecv.at[k], {"expert": c})
@@ -495,6 +529,18 @@
         copy.wait_send()
 
 
+def hand_over(*refs):
+    sems = refs[-1]
+    half = len(refs) // 2
+    copies = [
+        pltpu.make_async_copy(refs[i], refs[half + i], sems.at[i]) for i in range(half)
+    ]
+    for copy in copies:
+        copy.start()
+    for copy in copies:
+        copy.wait()
+
+
 def on_device_fused(
     tokens,
     cotangent,
@@ -513,35 +559,12 @@
     tok_count, width = tokens.shape
     ffl = w_gate.shape[2]
     rows = nd * CAP
-    flat = routes.reshape(-1)
-    order = jnp.arange(flat.shape[0], dtype=jnp.int32)
-    earlier = (flat[:, None] == flat[None, :]) & (order[None, :] < order[:, None])
-    rank = jnp.sum(earlier.astype(jnp.int32), axis=1)
-    place = (flat * CAP + rank).reshape(tok_count, TOP)
-    slot = jnp.arange(rows, dtype=jnp.int32)
-    hit0 = place[None, :, 0] == slot[:, None]
-    hit1 = place[None, :, 1] == slot[:, None]
-    pick = (hit0 | hit1).astype(jnp.bfloat16).reshape(nd, CAP, tok_count)
-    slotw = jnp.sum(
-        jnp.where(hit0, route_weight[None, :, 0], 0.0)
-        + jnp.where(hit1, route_weight[None, :, 1], 0.0),
-        axis=1,
-    ).reshape(nd, CAP, 1)
-    slot_tenant = jnp.sum(
-        jnp.where(hit0 | hit1, tenant[None, :].astype(jnp.float32), 0.0), axis=1
-    ).reshape(nd, 1, 1, CAP)
-    mine = (jnp.arange(nd, dtype=jnp.int32) == lax.axis_index("dp")).astype(jnp.float32)
-    tens = jnp.broadcast_to(slot_tenant * mine[None, None, :, None], (nd, 8, nd, CAP)).reshape(
-        nd, 8, rows
-    )
-    c0 = (place[:, 0:1] == slot[None, :]).astype(jnp.bfloat16)
-    c1 = (place[:, 1:2] == slot[None, :]).astype(jnp.bfloat16)
     vmem = pl.BlockSpec(memory_space=pltpu.VMEM)
     hbm = pl.BlockSpec(memory_space=pl.ANY)
     bf, f32 = jnp.bfloat16, jnp.float32
     dma = pltpu.SemaphoreType.DMA
     wide = TENANTS * RANK
-    mixed, gaut, gbu, gadt, gbd = pl.pallas_call(
+    results = pl.pallas_call(
         functools.partial(fused_kernel, nz, nd),
         out_shape=(
             jax.ShapeDtypeStruct((tok_count, width), bf),
@@ -550,9 +573,15 @@
             jax.ShapeDtypeStruct((wide, ffl), f32),
             jax.ShapeDtypeStruct((wide, width), f32),
         ),
-        in_specs=[vmem] * 8 + [hbm] * 3 + [vmem] * 4,
+        in_specs=[vmem] * 5 + [hbm] * 3 + [vmem] * 4,
         out_specs=[vmem] * 5,
         scratch_shapes=[
+            pltpu.VMEM((nd, CAP, tok_count), bf),
+            pltpu.VMEM((nd, CAP, tok_count), f32),
+            pltpu.VMEM((nd, 8, rows), f32),
+            pltpu.VMEM((tok_count, rows), bf),
+            pltpu.VMEM((tok_count, rows), bf),
+            pltpu.VMEM((TOP, tok_count, tok_count), f32),
             pltpu.VMEM((nz, width, ffl), bf),
             pltpu.VMEM((nz, width, ffl), bf),
             pltpu.VMEM((nz, ffl, width), bf),
@@ -593,12 +622,9 @@
     )(
         tokens,
         cotangent,
-        pick,
-        slotw,
-        tens,
-        c0,
-        c1,
-        route_weight,
+        routes.T,
+        route_weight.T,
+        tenant[None],
         w_gate,
         w_up,
         w_down,
@@ -607,6 +633,15 @@
         a_down[0].T,
         b_down[0],
     )
+    count = len(results)
+    mixed, gaut, gbu, gadt, gbd = pl.pallas_call(
+        hand_over,
+        out_shape=tuple(jax.ShapeDtypeStruct(r.shape, r.dtype) for r in results),
+        in_specs=[hbm] * count,
+        out_specs=[hbm] * count,
+        scratch_shapes=[dma((count,))],
+        compiler_params=pltpu.CompilerParams(vmem_limit_bytes=60 * 1024 * 1024),
+    )(*results)
     return mixed, gaut.T[None], gbu[None], gadt.T[None], gbd[None]
 
 

time: 105 us -> 139 us (1.32)
  Pallas kernels: 87.1 us -> 138 us
  local copies, waits for them, and re-layouts: 13.7 us -> 0 us
  other arithmetic: 3.22 us -> 0 us
    pallas_call x0 -> x1, Pallas kernels: none -> 50.8 us  [on_device_fused(): pl.pallas_call(hand_over, out_shape=tuple((jax.ShapeDtypeStruct(r.shape,...]
    unnamed x7 -> x0, local copies, waits for them, and re-layouts: 10.8 us -> none
    convert_element_type x4 -> x0, other arithmetic: 2.15 us -> none  [the longest x1 0.75 us: on_device_fused(): c0 = (place[:, 0:1] == slot[None, :]).astype(jnp.bfloat16)]
where the time goes in v2:
time: 139 us; the launch traced here: 138 us
  Pallas kernels  138 us (99%)
    pallas_call x1, Pallas kernels, on_device_fused(): pl.pallas_call(functools.partial(fused_kernel, nz, nd), out_shape=(jax.Sh...  87 us
    pallas_call x1, Pallas kernels, on_device_fused(): pl.pallas_call(hand_over, out_shape=tuple((jax.ShapeDtypeStruct(r.shape,...  50.8 us

profile of v2, /device:TPU:1, one launch (start us, length us, event | category | flops | bytes accessed | tf_op | source)
XLA Modules:
  0.0 138.4 jit_solution(3615044456204864911)
XLA Ops:
  0.6 87.0 %shard_map.155 = (bf16[128,768]{1,0:T(8,128)(2,1)}, f32[64,768]{1,0:T(8,128)}, f32[64,2048]{1,0:T(8,128)}, f32[64,2048]{1,0:T(8,128)}, f32[64,768]{1,0:T(8,128)}) custom-call(bf16[128,768]{1,0:T(8,128)(2,1)} %tok_ref.1, bf16[128,768]{1,0:T(8,128)(2,1)} %cot_ref.1, s32[2,128]{1,0:T(2,128)} %bitcast.23, f32[2,128]{1,0:T(2,128)} %bitcast.24, ...), custom_call_target="tpu_custom_call" | custom-call | tf_op jit(solution)/shard_map/pallas_call | solution.py:567
  87.6 50.8 %shard_map.156 = (bf16[128,768]{1,0:T(8,128)(2,1)}, f32[64,768]{1,0:T(8,128)}, f32[64,2048]{1,0:T(8,128)}, f32[64,2048]{1,0:T(8,128)}, f32[64,768]{1,0:T(8,128)}) custom-call(bf16[128,768]{1,0:T(8,128)(2,1)} %get-tuple-element.15.refs_0_, f32[64,768]{1,0:T(8,128)} %get-tuple-element.16.refs_1_, f32[64,2048]{1,0:T(8,128)} %get-tuple-element.17.refs_2_, ...), custom_call_target="tpu_custom_call" | custom-call | tf_op jit(solution)/shard_map/pallas_call | solution.py:637

commit v3 on v2

--- a/solution.py
+++ b/solution.py
@@ -229,6 +229,13 @@
     ds_ = [lax.rem(d + k, nd) for k in range(nd)]
     db = [lax.rem(d - k + nd, nd) for k in range(nd)]
     pending = []
+    below, above = z, nz - 1 - z
+    both = jnp.minimum(below, above)
+    longer = jnp.where(below > above, -1, 1)
+    near = [z]
+    for k in range(1, nz):
+        paired = (1 if k % 2 else -1) * ((k + 1) // 2)
+        near.append(z + jnp.where(k <= 2 * both, paired, longer * (k - both)))
 
     def remote(src, dst, ssem, rsem, dev):
         return pltpu.make_async_remote_copy(
@@ -266,13 +273,29 @@
         )
     pl.semaphore_wait(barrier, nz + nd - 2)
 
+    line_sends = []
+
+    def line_send(src, dst, which, s, up_way, may):
+        copy = remote(
+            src,
+            dst,
+            zsend.at[which, s, up_way],
+            zrecv.at[which, s],
+            {"expert": lax.rem(z + nz + 2 * up_way - 1, nz)},
+        )
+        line_sends.append((copy, may))
+        pl.when(may)(copy.start)
+
+    def own_line(which):
+        own, gathered = ((tok_ref, tokg), (cot_ref, cotg))[which]
+        line_send(own, gathered.at[z], which, z, 0, z > 0)
+        line_send(own, gathered.at[z], which, z, 1, z < nz - 1)
+
+    own_line(0)
+
     for k in range(1, nz):
-        send(tok_ref, tokg.at[z], zsend.at[0, k], zrecv.at[0, k], {"expert": zs[k]})
-    for k in range(1, nz):
-        send(cot_ref, cotg.at[z], zsend.at[1, k], zrecv.at[1, k], {"expert": zs[k]})
-    for k in range(1, nz):
-        weight(0, zb[k]).start()
-        weight(1, zb[k]).start()
+        weight(0, near[k]).start()
+        weight(1, near[k]).start()
     for k in range(nz):
         weight(2, zs[(k + 1) % nz]).start()
 
@@ -310,14 +333,18 @@
         send(tens_ref.at[k], tenr.at[d], tsend.at[k], trecv.at[k], {"dp": ds_[k]})
 
     def dispatch(which, j):
-        s = zb[j]
+        s = near[j]
         own, gathered, sel, buf = (
             (tok_ref, tokg, selx, xbuf) if which == 0 else (cot_ref, cotg, seld, dbuf)
         )
         if j:
             remote(
-                own, gathered.at[s], zsend.at[which, j], zrecv.at[which, j], {"expert": zs[j]}
+                own, gathered.at[s], zsend.at[which, s, 0], zrecv.at[which, s], {"expert": zs[1]}
             ).wait_recv()
+            line_send(gathered.at[s], gathered.at[s], which, s, 0, (s > z) & (z > 0))
+            line_send(gathered.at[s], gathered.at[s], which, s, 1, (s < z) & (z < nz - 1))
+            if which == 0 and j == nz - 2:
+                own_line(1)
             block = gathered[s]
         else:
             block = own[...]
@@ -340,7 +367,7 @@
                 buf[s, d] = picked
 
     def arrived(which, j):
-        s = zb[j]
+        s = near[j]
         sel, buf = (selx, xbuf) if which == 0 else (seld, dbuf)
         for k in range(1, nd):
             remote(
@@ -527,18 +554,14 @@
     mixed_ref[...] = total.astype(jnp.bfloat16)
     for copy in pending:
         copy.wait_send()
+    for copy, may in line_sends:
+        pl.when(may)(copy.wait_send)
 
 
 def hand_over(*refs):
-    sems = refs[-1]
     half = len(refs) // 2
-    copies = [
-        pltpu.make_async_copy(refs[i], refs[half + i], sems.at[i]) for i in range(half)
-    ]
-    for copy in copies:
-        copy.start()
-    for copy in copies:
-        copy.wait()
+    for i in range(half):
+        refs[half + i][...] = refs[i][...]
 
 
 def on_device_fused(
@@ -603,7 +626,7 @@
             pltpu.VMEM((nd, 8, rows), f32),
             pltpu.VMEM((4, nz, RANK, rows), f32),
             dma((3, nz)),
-            dma((2, nz)),
+            dma((2, nz, 2)),
             dma((2, nz)),
             dma((2, nz, nd)),
             dma((2, nz, nd)),
@@ -637,10 +660,8 @@
     mixed, gaut, gbu, gadt, gbd = pl.pallas_call(
         hand_over,
         out_shape=tuple(jax.ShapeDtypeStruct(r.shape, r.dtype) for r in results),
-        in_specs=[hbm] * count,
-        out_specs=[hbm] * count,
-        scratch_shapes=[dma((count,))],
-        compiler_params=pltpu.CompilerParams(vmem_limit_bytes=60 * 1024 * 1024),
+        in_specs=[vmem] * count,
+        out_specs=[vmem] * count,
     )(*results)
     return mixed, gaut.T[None], gbu[None], gadt.T[None], gbd[None]
 

time: 139 us -> 83.6 us (0.60)
  Pallas kernels: 138 us -> 82.8 us
    pallas_call x1, Pallas kernels: 50.8 us -> 2.57 us  [on_device_fused(): pl.pallas_call(hand_over, out_shape=tuple((jax.ShapeDtypeStruct(r.shape,...]
    pallas_call x1, Pallas kernels: 87 us -> 80.2 us  [on_device_fused(): pl.pallas_call(functools.partial(fused_kernel, nz, nd), out_shape=(jax.Sh...]
where the time goes in v3:
time: 83.6 us; the launch traced here: 83.4 us
  Pallas kernels  82.8 us (99%)
    pallas_call x1, Pallas kernels, on_device_fused(): pl.pallas_call(functools.partial(fused_kernel, nz, nd), out_shape=(jax.Sh...  80.2 us
    pallas_call x1, Pallas kernels, on_device_fused(): pl.pallas_call(hand_over, out_shape=tuple((jax.ShapeDtypeStruct(r.shape,...  2.57 us

profile of v3, /device:TPU:1, one launch (start us, length us, event | category | flops | bytes accessed | tf_op | source)
XLA Modules:
  0.0 83.4 jit_solution(1923241931837026696)
XLA Ops:
  0.6 80.2 %shard_map.155 = (bf16[128,768]{1,0:T(8,128)(2,1)}, f32[64,768]{1,0:T(8,128)}, f32[64,2048]{1,0:T(8,128)}, f32[64,2048]{1,0:T(8,128)}, f32[64,768]{1,0:T(8,128)}) custom-call(bf16[128,768]{1,0:T(8,128)(2,1)} %tok_ref.1, bf16[128,768]{1,0:T(8,128)(2,1)} %cot_ref.1, s32[2,128]{1,0:T(2,128)} %bitcast.23, f32[2,128]{1,0:T(2,128)} %bitcast.24, ...), custom_call_target="tpu_custom_call" | custom-call | tf_op jit(solution)/shard_map/pallas_call | solution.py:590
  80.9 2.6 %shard_map.156 = (bf16[128,768]{1,0:T(8,128)(2,1)}, f32[64,768]{1,0:T(8,128)}, f32[64,2048]{1,0:T(8,128)}, f32[64,2048]{1,0:T(8,128)}, f32[64,768]{1,0:T(8,128)}) custom-call(bf16[128,768]{1,0:T(8,128)(2,1)} %get-tuple-element.15.refs_0_, f32[64,768]{1,0:T(8,128)} %get-tuple-element.16.refs_1_, f32[64,2048]{1,0:T(8,128)} %get-tuple-element.17.refs_2_, ...), custom_call_target="tpu_custom_call" | custom-call | tf_op jit(solution)/shard_map/pallas_call | solution.py:660
